TPU v7x, 256 devices: a whole 4x4x8 slice. The times are simulated.
256 devices in a mesh: dp: 32 (over y, z), tensor: 8 (over x, core).
Axes of the slice: x: 4, y: 4, z: 8, core: 2. Of those that a mesh axis runs over, the one named last changes fastest.
Arguments:
- queries: bfloat16 [8192, 8192], P('dp', 'tensor')
- keys: bfloat16 [8192, 1024], P('dp', 'tensor')
- values: bfloat16 [8192, 1024], P('dp', 'tensor'), may hold values from -6 to 6
- prompt_keys: bfloat16 [4096, 1024], P('dp', 'tensor'), may hold values from -6 to 6
- prompt_values: bfloat16 [4096, 1024], P('dp', 'tensor'), may hold values from -6 to 6
- lengths: int32 [32, 4], P('dp'), may hold values from 1 to 128, 256 in all within a row
- owner_slice: int32 [32], replicated, may hold values from 0 to 31, each once
- device_group: int32 [32], replicated, may hold values from 0 to 7
- out_weight: bfloat16 [8192, 5120], P('tensor'), may hold values from -0.0625 to 0.0625
- cotangent: bfloat16 [8192, 5120], P('dp', 'tensor'), may hold values from -6 to 6
Outputs:
- block_out: bfloat16 [8192, 5120], P(('dp', 'tensor'))
- grad_queries: bfloat16 [8192, 8192], P('dp', 'tensor')
- grad_keys: bfloat16 [8192, 1024], P('dp', 'tensor')
- grad_values: bfloat16 [8192, 1024], P('dp', 'tensor')
- grad_prompt_keys: float32 [4096, 1024], P('dp', 'tensor')
- grad_prompt_values: float32 [4096, 1024], P('dp', 'tensor')
Inputs may be any that keep to these rules, and one draw needn't show every extreme that they name: Each row holds 4 lengths that sum to 256; its largest is exactly half of 256. `owner_slice`: a permutation of the 32 prompt slices.
All inputs are finite; a program needn't handle non-finite values.
Results may differ from a plain program's by a relative error of at most 0.034.
Values may be sent and summed in bfloat16 or wider, within the bound.
A program may use at most 128 MiB of HBM per device.

v0:
```python
import functools

import jax
import jax.numpy as jnp
from jax import lax
from jax.experimental import pallas as pl
from jax.experimental.pallas import tpu as pltpu
from jax.sharding import PartitionSpec as P

Y, Z, X = 4, 8, 4
HEAD = 128
HEADS = 8
ROWS = 256
PROMPT = 512
KEYS = PROMPT + ROWS
D = 5120
BLK = D // 8
PAIR = 2 * BLK
CH = 4
CW = D // CH
SCALE = HEAD**-0.5
EXP_SCALE = SCALE * 1.4426950408889634
MASKED = -1e30 / SCALE
MESH = pl.DeviceIdType.MESH
F32, BF16 = jnp.float32, jnp.bfloat16
NT = (((1,), (1,)), ((), ()))
NN = (((1,), (0,)), ((), ()))


def dot(a, b, dims=NN):
    return lax.dot_general(a, b, dims, preferred_element_type=F32)


def kernel(
    len_s, own_s, grp_s,
    q_h, k_h, v_h, pk_h, pv_h, w_h, cot_h,
    bo_h, gq_h, gk_h, gv_h, gpk_h, gpv_h,
    w_s, cot_s, ga_acc, ga_t, q3, kall, vall, kt_s, vt_s, parts_k, parts_v, pick_k, pick_v,
    mask_s, pt_s, ds_s, ga_n, inverse_s, delta_s, att_s, gq_s, gkv_s,
    g_k, g_v, rg_k, rg_v, qs_k, qs_v, rq_k, rq_v, u_k, u_v, fin_k, fin_v, out_k, out_v,
    pb, rb1, acc, rs1, rs2, bo_s, inv_s,
    loc, z1s, z1r, y2s, y2r, z3s, z3r, xs, xr, ps, pr,
    b3s, b3r, b2s, b2r, b1s, b1r, cs, cr, r1s, r1r, r2s, r2r,
):
    me = lax.axis_index("dp")
    t = lax.axis_index("tensor")
    y, z = me // Z, me % Z
    x, c = t // 2, t % 2
    right = lax.rem(x + 1, X)
    left = lax.rem(x + X - 1, X)
    opp = lax.rem(x + 2, X)

    def at_z(d):
        return (y * Z + lax.rem(z + d, Z), t)

    def at_y(d):
        return (lax.rem(y + d, Y) * Z + z, t)

    to_right = (me, right * 2 + c)
    to_left = (me, left * 2 + c)
    partner = (me, x * 2 + 1 - c)
    sent = []

    def send(src, dst, ss, rs, dev):
        cp = pltpu.make_async_remote_copy(
            src_ref=src, dst_ref=dst, send_sem=ss, recv_sem=rs, device_id=dev, device_id_type=MESH
        )
        cp.start()
        sent.append(cp)
        return cp

    lane = pl.ds(pl.multiple_of(c * BLK, 128), BLK)
    loads = [
        pltpu.make_async_copy(pk_h.at[z], parts_k.at[me], loc.at[3]),
        pltpu.make_async_copy(pv_h.at[z], parts_v.at[me], loc.at[4]),
        pltpu.make_async_copy(cot_h, cot_s.at[x, :, lane], loc.at[0]),
        pltpu.make_async_copy(k_h, kall.at[pl.ds(4, 2)], loc.at[1]),
        pltpu.make_async_copy(v_h, vall.at[pl.ds(4, 2)], loc.at[2]),
        pltpu.make_async_copy(w_h, w_s, loc.at[5]),
    ]
    for h in range(HEADS):
        loads.append(
            pltpu.make_async_copy(q_h.at[:, pl.ds(h * HEAD, HEAD)], q3.at[h], loc.at[6 + h])
        )
    for cp in loads:
        cp.start()

    barrier = pltpu.get_barrier_semaphore()
    peers = [at_z(d) for d in range(1, Z)] + [at_y(d) for d in range(1, Y)]
    peers += [to_right, to_left, partner]
    for dev in peers:
        pl.semaphore_signal(barrier, inc=1, device_id=dev, device_id_type=MESH)
    pl.semaphore_wait(barrier, len(peers))

    z1 = []
    for kv, (src, dst) in enumerate(((pk_h, parts_k), (pv_h, parts_v))):
        z1.append(
            [
                send(src.at[lax.rem(z + d, Z)], dst.at[me], z1s.at[kv, d], z1r.at[kv, d], at_z(d))
                for d in range(1, Z)
            ]
        )
    lo, hi = pl.ds(0, 128), pl.ds(128, 128)
    own_cot = cot_s.at[x]
    ra = send(cot_h.at[lo], own_cot.at[lo, lane], xs.at[0], xr.at[0], to_right)
    lb = send(cot_h.at[hi], own_cot.at[hi, lane], xs.at[1], xr.at[1], to_left)
    rb = send(cot_h.at[hi], own_cot.at[hi, lane], xs.at[2], xr.at[2], to_right)
    la = send(cot_h.at[lo], own_cot.at[lo, lane], xs.at[3], xr.at[3], to_left)
    p_own = send(cot_h, own_cot.at[:, lane], ps.at[0], pr.at[0], partner)

    def find(s, _):
        def scan(j, found):
            return jnp.where(own_s[j] == s, j, found)

        inv_s[s] = lax.fori_loop(0, Y * Z, scan, jnp.int32(0), unroll=True)
        return 0

    lax.fori_loop(0, Y * Z, find, 0)

    key_at = lax.broadcasted_iota(jnp.int32, (ROWS, ROWS), 0)
    query_at = lax.broadcasted_iota(jnp.int32, (ROWS, ROWS), 1)
    end0 = len_s[0, 0]
    end1 = end0 + len_s[0, 1]
    end2 = end1 + len_s[0, 2]

    def segment(at):
        return (
            (at >= end0).astype(jnp.int32)
            + (at >= end1).astype(jnp.int32)
            + (at >= end2).astype(jnp.int32)
        )

    seen = (segment(key_at) == segment(query_at)) & (key_at <= query_at)
    mask_s[...] = seen.astype(jnp.int32)

    def forward(block, rows, s):
        ref = cot_s.at[block, rows, lane]
        return send(ref, ref, ps.at[s], pr.at[s], partner)

    def grad_att(block, first=False, last=False):
        cols = pl.ds(pl.multiple_of(block * PAIR, 128), PAIR)
        part = dot(w_s[:, cols], cot_s[block], NT)
        if first:
            ga_acc[...] = part
        elif last:
            ga_t[...] = (ga_acc[...] + part).astype(BF16).reshape(HEADS, HEAD, ROWS)
        else:
            ga_acc[...] += part

    y2 = []
    for kv, ref in enumerate((parts_k, parts_v)):
        loads[kv].wait()
        for cp in z1[kv]:
            cp.wait_recv()
        rows = ref.at[pl.ds(y * Z, Z)]
        y2.append([send(rows, rows, y2s.at[kv, d], y2r.at[kv, d], at_y(d)) for d in range(1, Y)])

    ra.wait_recv()
    ref = cot_s.at[left, lo, lane]
    fr = send(ref, ref, xs.at[4], xr.at[4], to_right)
    lb.wait_recv()
    ref = cot_s.at[right, hi, lane]
    fl = send(ref, ref, xs.at[5], xr.at[5], to_left)
    p_la = forward(left, lo, 1)
    p_rb = forward(right, hi, 2)

    loads[2].wait()
    loads[5].wait()
    p_own.wait_recv()
    grad_att(x, first=True)

    z3 = []
    for kv, (ref, pick, full) in enumerate(((parts_k, pick_k, kall), (parts_v, pick_v, vall))):
        for cp in y2[kv]:
            cp.wait_recv()

        def choose(dest, _, ref=ref, pick=pick):
            first = grp_s[y * Z + dest] * 4
            for p in range(4):
                pick[dest, p] = ref[inv_s[first + p]]
            return 0

        lax.fori_loop(0, Z, choose, 0, unroll=True)
        copies = []
        for d in range(1, Z):
            dest = lax.rem(z + d, Z)
            copies.append(
                send(
                    pick.at[dest], full.at[pl.ds(0, 4), z], z3s.at[kv, d], z3r.at[kv, d], at_z(d)
                )
            )
        for p in range(4):
            full[p, z] = pick[z, p]
        z3.append(copies)

    rb.wait_recv()
    p_lb = forward(left, hi, 3)
    la.wait_recv()
    p_ra = forward(right, lo, 4)
    p_la.wait_recv()
    p_lb.wait_recv()
    grad_att(left)
    fr.wait_recv()
    p_oa = forward(opp, lo, 5)
    fl.wait_recv()
    p_ob = forward(opp, hi, 6)
    p_rb.wait_recv()
    p_ra.wait_recv()
    grad_att(right)

    for cp in loads[3:5] + loads[6:]:
        cp.wait()
    for cp in z3[0]:
        cp.wait_recv()
    kt_s[...] = kall[...].reshape(KEYS, HEAD).T

    def queries_of(h):
        return pl.ds(pl.multiple_of(h * ROWS, ROWS), ROWS)

    def features_of(h):
        return pl.ds(pl.multiple_of(h * HEAD, HEAD), HEAD)

    def score_head(h, _):
        st = dot(kall[...].reshape(KEYS, HEAD), q3[h], NT)
        s0 = st[:PROMPT]
        s1 = jnp.where(mask_s[...] != 0, st[PROMPT:], MASKED)
        top = jnp.maximum(jnp.max(s0, 0, keepdims=True), jnp.max(s1, 0, keepdims=True))
        e0 = jnp.exp2((s0 - top) * EXP_SCALE)
        e1 = jnp.exp2((s1 - top) * EXP_SCALE)
        total = jnp.sum(e0, 0, keepdims=True) + jnp.sum(e1, 0, keepdims=True)
        inverse_s[h] = 1.0 / total
        pt_s[:PROMPT, queries_of(h)] = e0.astype(BF16)
        pt_s[PROMPT:, queries_of(h)] = e1.astype(BF16)
        return 0

    lax.fori_loop(0, HEADS, score_head, 0, unroll=True)

    p_oa.wait_recv()
    p_ob.wait_recv()
    grad_att(opp, last=True)

    for cp in z3[1]:
        cp.wait_recv()
    vt_s[...] = vall[...].reshape(KEYS, HEAD).T

    def value_head(h, _):
        inverse = inverse_s[h]
        out_t = dot(vt_s[...], pt_s[:, queries_of(h)]) * inverse
        low = out_t.astype(BF16).astype(F32)
        grad = ga_t[h].astype(F32)
        delta_s[h] = jnp.sum(low * grad, 0, keepdims=True) * inverse
        ga_n[:, queries_of(h)] = (grad * inverse).astype(BF16)
        att_s[:, features_of(h)] = out_t.T.astype(BF16)
        return 0

    lax.fori_loop(0, HEADS, value_head, 0, unroll=True)

    def reduce_start(kv, grad, g_ref, rg):
        g_ref[...] = grad[:PROMPT].astype(BF16).reshape(4, Z, 16, HEAD)
        rg[z] = g_ref[:, z]
        return [
            send(
                g_ref.at[:, lax.rem(z + d, Z)], rg.at[z], b3s.at[kv, d], b3r.at[kv, d], at_z(d)
            )
            for d in range(1, Z)
        ]

    b3 = [None, None]
    b2 = [None, None]
    b1 = [None, None]
    grad_v = dot(pt_s[...], ga_n[...], NT)
    b3[1] = reduce_start(1, grad_v, g_v, rg_v)
    gkv_s[1] = grad_v[PROMPT:].astype(BF16)
    stores = [pltpu.make_async_copy(gkv_s.at[1], gv_h, loc.at[14])]
    stores[-1].start()

    def backward_head(h, _):
        grad_p = dot(vall[...].reshape(KEYS, HEAD), ga_n[:, queries_of(h)])
        probs = pt_s[:, queries_of(h)].astype(F32)
        ds_s[:, queries_of(h)] = (probs * (grad_p - delta_s[h])).astype(BF16)
        return 0

    lax.fori_loop(0, HEADS, backward_head, 0, unroll=True)
    grad_k = dot(ds_s[...], q3[...].reshape(HEADS * ROWS, HEAD)) * SCALE
    b3[0] = reduce_start(0, grad_k, g_k, rg_k)
    gkv_s[0] = grad_k[PROMPT:].astype(BF16)
    stores.append(pltpu.make_async_copy(gkv_s.at[0], gk_h, loc.at[15]))
    stores[-1].start()

    def query_head(h, _):
        dq = dot(kt_s[...], ds_s[:, queries_of(h)])
        gq_s[:, features_of(h)] = (dq.T * SCALE).astype(BF16)
        return 0

    def reduce_z(kv, rg, qs, rq):
        for cp in b3[kv]:
            cp.wait_recv()

        def slot(j, _):
            s = own_s[j]
            group, piece = s // 4, s % 4
            total = jnp.zeros((16, HEAD), F32)
            for source in range(Z):
                hit = jnp.full((16, HEAD), grp_s[y * Z + source], jnp.int32) == group
                total += jnp.where(hit, rg[source, piece].astype(F32), 0.0)
            qs[j] = total.astype(BF16)
            return 0

        lax.fori_loop(0, Y * Z, slot, 0, unroll=4)
        rq[y] = qs[pl.ds(y * Z, Z)]
        b2[kv] = [
            send(
                qs.at[pl.ds(lax.rem(y + d, Y) * Z, Z)],
                rq.at[y],
                b2s.at[kv, d],
                b2r.at[kv, d],
                at_y(d),
            )
            for d in range(1, Y)
        ]

    def reduce_y(kv, rq, u, fin):
        for cp in b2[kv]:
            cp.wait_recv()
        total = rq[0].astype(F32)
        for source in range(1, Y):
            total += rq[source].astype(F32)
        u[...] = total.astype(BF16)
        fin[z] = u[z]
        b1[kv] = [
            send(u.at[lax.rem(z + d, Z)], fin.at[z], b1s.at[kv, d], b1r.at[kv, d], at_z(d))
            for d in range(1, Z)
        ]

    def reduce_end(kv, fin, out, dst):
        for cp in b1[kv]:
            cp.wait_recv()
        out[...] = fin[...].astype(F32)
        stores.append(pltpu.make_async_copy(out, dst, loc.at[17 + kv]))
        stores[-1].start()

    core = [None] * CH
    one = [None] * CH
    two = [None] * CH

    def product(n):
        part = dot(att_s[...], w_s[:, n * CW : (n + 1) * CW])
        pb[n] = part.astype(BF16).reshape(X, 2, 32, CW)
        core[n] = send(pb.at[n, :, 1 - c], rb1.at[n], cs.at[n], cr.at[n], partner)

    def ring_one(n):
        core[n].wait_recv()
        for d in range(X):
            b = lax.rem(x + d, X)
            acc[n, d] = (pb[n, b, c].astype(F32) + rb1[n, b].astype(F32)).astype(BF16)
        one[n] = (
            send(acc.at[n, 2, pl.ds(0, 16)], rs1.at[n, 0], r1s.at[n, 0], r1r.at[n, 0], to_right),
            send(acc.at[n, 2, pl.ds(16, 16)], rs1.at[n, 1], r1s.at[n, 1], r1r.at[n, 1], to_left),
        )

    def ring_two(n):
        one[n][0].wait_recv()
        acc[n, 1, :16] = (acc[n, 1, :16].astype(F32) + rs1[n, 0].astype(F32)).astype(BF16)
        first = send(acc.at[n, 1], rs2.at[n, 0], r2s.at[n, 0], r2r.at[n, 0], to_right)
        one[n][1].wait_recv()
        acc[n, 3, 16:] = (acc[n, 3, 16:].astype(F32) + rs1[n, 1].astype(F32)).astype(BF16)
        two[n] = (
            first,
            send(acc.at[n, 3], rs2.at[n, 1], r2s.at[n, 1], r2r.at[n, 1], to_left),
        )

    def ring_end(n):
        two[n][0].wait_recv()
        two[n][1].wait_recv()
        total = acc[n, 0].astype(F32) + rs2[n, 0].astype(F32) + rs2[n, 1].astype(F32)
        bo_s[:, n * CW : (n + 1) * CW] = total.astype(BF16)

    product(0)
    product(1)
    ring_one(0)
    product(2)
    ring_one(1)
    product(3)
    lax.fori_loop(0, HEADS, query_head, 0, unroll=True)
    stores.append(pltpu.make_async_copy(gq_s, gq_h, loc.at[16]))
    stores[-1].start()
    reduce_z(1, rg_v, qs_v, rq_v)
    ring_one(2)
    ring_one(3)
    ring_two(0)
    reduce_z(0, rg_k, qs_k, rq_k)
    ring_two(1)
    reduce_y(1, rq_v, u_v, fin_v)
    ring_two(2)
    ring_two(3)
    reduce_y(0, rq_k, u_k, fin_k)
    early = len(sent)
    for cp in sent[: early - 2 * Z]:
        cp.wait_send()
    ring_end(0)
    ring_end(1)
    reduce_end(1, fin_v, out_v, gpv_h)
    ring_end(2)
    ring_end(3)
    stores.append(pltpu.make_async_copy(bo_s, bo_h, loc.at[19]))
    stores[-1].start()
    reduce_end(0, fin_k, out_k, gpk_h)
    for cp in sent[early - 2 * Z :]:
        cp.wait_send()
    for cp in stores:
        cp.wait()


def place(*refs):
    ins, outs, held, (taken, given) = refs[:6], refs[6:12], refs[12:18], refs[18:]
    loads = [pltpu.make_async_copy(a, b, taken.at[i]) for i, (a, b) in enumerate(zip(ins, held))]
    stores = [pltpu.make_async_copy(a, b, given.at[i]) for i, (a, b) in enumerate(zip(held, outs))]
    for cp in loads:
        cp.start()
    for load, store in zip(loads, stores):
        load.wait()
        store.start()
    for cp in stores:
        cp.wait()


def local(
    queries, keys, values, prompt_keys, prompt_values,
    lengths, owner_slice, device_group, out_weight, cotangent,
):
    smem = pl.BlockSpec(memory_space=pltpu.SMEM)
    hbm = pl.BlockSpec(memory_space=pl.ANY)
    vm = pltpu.VMEM
    dma = pltpu.SemaphoreType.DMA
    tile = (16, HEAD)
    scratch = [
        vm((HEADS * HEAD, D), BF16),
        vm((X, ROWS, PAIR), BF16),
        vm((HEADS * HEAD, ROWS), F32),
        vm((HEADS, HEAD, ROWS), BF16),
        vm((HEADS, ROWS, HEAD), BF16),
        vm((6, Z) + tile, BF16),
        vm((6, Z) + tile, BF16),
        vm((HEAD, KEYS), BF16),
        vm((HEAD, KEYS), BF16),
        vm((Y * Z,) + tile, BF16),
        vm((Y * Z,) + tile, BF16),
        vm((Z, 4) + tile, BF16),
        vm((Z, 4) + tile, BF16),
        vm((ROWS, ROWS), jnp.int32),
        vm((KEYS, HEADS * ROWS), BF16),
        vm((KEYS, HEADS * ROWS), BF16),
        vm((HEAD, HEADS * ROWS), BF16),
        vm((HEADS, 1, ROWS), F32),
        vm((HEADS, 1, ROWS), F32),
        vm((ROWS, HEADS * HEAD), BF16),
        vm((ROWS, HEADS * HEAD), BF16),
        vm((2, ROWS, HEAD), BF16),
        vm((4, Z) + tile, BF16),
        vm((4, Z) + tile, BF16),
        vm((Z, 4) + tile, BF16),
        vm((Z, 4) + tile, BF16),
        vm((Y * Z,) + tile, BF16),
        vm((Y * Z,) + tile, BF16),
        vm((Y, Z) + tile, BF16),
        vm((Y, Z) + tile, BF16),
        vm((Z,) + tile, BF16),
        vm((Z,) + tile, BF16),
        vm((Z,) + tile, BF16),
        vm((Z,) + tile, BF16),
        vm((Z,) + tile, F32),
        vm((Z,) + tile, F32),
        vm((CH, X, 2, 32, CW), BF16),
        vm((CH, X, 32, CW), BF16),
        vm((CH, X, 32, CW), BF16),
        vm((CH, 2, 16, CW), BF16),
        vm((CH, 2, 32, CW), BF16),
        vm((32, D), BF16),
        pltpu.SMEM((Y * Z,), jnp.int32),
        dma((20,)),
        dma((2, Z)), dma((2, Z)),
        dma((2, Y)), dma((2, Y)),
        dma((2, Z)), dma((2, Z)),
        dma((6,)), dma((6,)),
        dma((7,)), dma((7,)),
        dma((2, Z)), dma((2, Z)),
        dma((2, Y)), dma((2, Y)),
        dma((2, Z)), dma((2, Z)),
        dma((CH,)), dma((CH,)),
        dma((CH, 2)), dma((CH, 2)),
        dma((CH, 2)), dma((CH, 2)),
    ]
    shape = jax.ShapeDtypeStruct
    outs = pl.pallas_call(
        kernel,
        out_shape=(
            shape((32, D), BF16),
            shape((ROWS, HEADS * HEAD), BF16),
            shape((ROWS, HEAD), BF16),
            shape((ROWS, HEAD), BF16),
            shape((Z,) + tile, F32),
            shape((Z,) + tile, F32),
        ),
        in_specs=[smem] * 3 + [hbm] * 7,
        out_specs=[hbm] * 6,
        scratch_shapes=scratch,
        compiler_params=pltpu.CompilerParams(
            collective_id=0, has_side_effects=True, vmem_limit_bytes=58 * 1024 * 1024
        ),
        name="attention_block",
    )(
        lengths,
        owner_slice,
        device_group,
        queries,
        keys.reshape(2, Z, 16, HEAD),
        values.reshape(2, Z, 16, HEAD),
        prompt_keys.reshape(Z, 16, HEAD),
        prompt_values.reshape(Z, 16, HEAD),
        out_weight,
        cotangent,
    )
    outs = pl.pallas_call(
        place,
        out_shape=tuple(shape(o.shape, o.dtype) for o in outs),
        in_specs=[hbm] * 6,
        out_specs=[hbm] * 6,
        scratch_shapes=[vm(o.shape, o.dtype) for o in outs] + [dma((6,)), dma((6,))],
        name="place",
    )(*outs)
    return outs[:4] + (outs[4].reshape(128, HEAD), outs[5].reshape(128, HEAD))


def solution(mesh):
    placed = (
        P("dp", "tensor"),
        P("dp", "tensor"),
        P("dp", "tensor"),
        P("dp", "tensor"),
        P("dp", "tensor"),
        P("dp", None),
        P(),
        P(),
        P("tensor", None),
        P("dp", "tensor"),
    )
    return jax.shard_map(
        local,
        mesh=mesh,
        in_specs=placed,
        out_specs=(
            P(("dp", "tensor"), None),
            P("dp", "tensor"),
            P("dp", "tensor"),
            P("dp", "tensor"),
            P("dp", "tensor"),
            P("dp", "tensor"),
        ),
        check_vma=False,
    )
```

profile of v0, /device:TPU:1, one launch (start us, length us, event | category | flops | bytes accessed | tf_op | source)
XLA Modules:
  0.0 59.9 jit_solution(6391474167587846741)
XLA Ops:
  0.6 57.1 %attention_block.1 = (bf16[32,5120]{1,0:T(8,128)(2,1)}, bf16[256,1024]{1,0:T(8,128)(2,1)}, bf16[256,128]{1,0:T(8,128)(2,1)}, bf16[256,128]{1,0:T(8,128)(2,1)}, f...) custom-call(s32[1,4]{1,0:T(1,128)} %len_s.1, s32[32]{0:T(128)} %own_s.1, s32[32]{0:T(128)} %grp_s.1, bf16[256,1024]{1,0:T(8,128)(2,1)} %q_h.1, ...), custom_call_target="tpu_custom_call" | custom-call | tf_op jit(solution)/shard_map/attention_block/pallas_call | solution.py:494
  57.8 2.1 %place.1 = (bf16[32,5120]{1,0:T(8,128)(2,1)}, bf16[256,1024]{1,0:T(8,128)(2,1)}, bf16[256,128]{1,0:T(8,128)(2,1)}, bf16[256,128]{1,0:T(8,128)(2,1)}, f32[8,16,128]{2,1,0:T(8,128)}, /*index=5*/f32[8,16,128]{2,1,0:T(8,128)}) custom-call(bf16[32,5120]{1,0:T(8,128)(2,1)} %get-tuple-element.18.refs_0_, bf16[256,1024]{1,0:T(8,128)(2,1)} %get-tuple-element.19.refs_1_, ...), custom_call_target="tpu_custom_call" | custom-call | tf_op jit(solution)/shard_map/place/pallas_call | solution.py:523
where the time goes:
time: 60 us; the launch traced here: 59.9 us
  Pallas kernels  59.2 us (99%)
  between operations  0.64 us (1%)
    pallas_call x1, Pallas kernels, local(): pl.pallas_call(kernel, out_shape=(shape((32, D), BF16), shape((ROWS, HEAD...  57.1 us
    pallas_call x1, Pallas kernels, local(): pl.pallas_call(place, out_shape=tuple((shape(o.shape, o.dtype) for o in o...  2.12 us

commit v1 on v0

--- a/solution.py
+++ b/solution.py
@@ -35,9 +35,9 @@
     len_s, own_s, grp_s,
     q_h, k_h, v_h, pk_h, pv_h, w_h, cot_h,
     bo_h, gq_h, gk_h, gv_h, gpk_h, gpv_h,
-    w_s, cot_s, ga_acc, ga_t, q3, kall, vall, kt_s, vt_s, parts_k, parts_v, pick_k, pick_v,
+    pk_s, pv_s, w_s, cot_s, ga_acc, ga_t, q3, kall, vall, kt_s, vt_s, parts_k, parts_v, pick_k, pick_v,
     mask_s, pt_s, ds_s, ga_n, inverse_s, delta_s, att_s, gq_s, gkv_s,
-    g_k, g_v, rg_k, rg_v, qs_k, qs_v, rq_k, rq_v, u_k, u_v, fin_k, fin_v, out_k, out_v,
+    g_k, g_v, rg_k, rg_v, qs_k, qs_v, rq_k, rq_v, u_k, u_v, so_s, top_s,
     pb, rb1, acc, rs1, rs2, bo_s, inv_s,
     loc, z1s, z1r, y2s, y2r, z3s, z3r, xs, xr, ps, pr,
     b3s, b3r, b2s, b2r, b1s, b1r, cs, cr, r1s, r1r, r2s, r2r,
@@ -71,8 +71,8 @@
 
     lane = pl.ds(pl.multiple_of(c * BLK, 128), BLK)
     loads = [
-        pltpu.make_async_copy(pk_h.at[z], parts_k.at[me], loc.at[3]),
-        pltpu.make_async_copy(pv_h.at[z], parts_v.at[me], loc.at[4]),
+        pltpu.make_async_copy(pk_h, pk_s, loc.at[3]),
+        pltpu.make_async_copy(pv_h, pv_s, loc.at[4]),
         pltpu.make_async_copy(cot_h, cot_s.at[x, :, lane], loc.at[0]),
         pltpu.make_async_copy(k_h, kall.at[pl.ds(4, 2)], loc.at[1]),
         pltpu.make_async_copy(v_h, vall.at[pl.ds(4, 2)], loc.at[2]),
@@ -82,7 +82,7 @@
         loads.append(
             pltpu.make_async_copy(q_h.at[:, pl.ds(h * HEAD, HEAD)], q3.at[h], loc.at[6 + h])
         )
-    for cp in loads:
+    for cp in loads[:3]:
         cp.start()
 
     barrier = pltpu.get_barrier_semaphore()
@@ -93,7 +93,8 @@
     pl.semaphore_wait(barrier, len(peers))
 
     z1 = []
-    for kv, (src, dst) in enumerate(((pk_h, parts_k), (pv_h, parts_v))):
+    for kv, (src, dst) in enumerate(((pk_s, parts_k), (pv_s, parts_v))):
+        loads[kv].wait()
         z1.append(
             [
                 send(src.at[lax.rem(z + d, Z)], dst.at[me], z1s.at[kv, d], z1r.at[kv, d], at_z(d))
@@ -102,11 +103,21 @@
         )
     lo, hi = pl.ds(0, 128), pl.ds(128, 128)
     own_cot = cot_s.at[x]
-    ra = send(cot_h.at[lo], own_cot.at[lo, lane], xs.at[0], xr.at[0], to_right)
-    lb = send(cot_h.at[hi], own_cot.at[hi, lane], xs.at[1], xr.at[1], to_left)
-    rb = send(cot_h.at[hi], own_cot.at[hi, lane], xs.at[2], xr.at[2], to_right)
-    la = send(cot_h.at[lo], own_cot.at[lo, lane], xs.at[3], xr.at[3], to_left)
-    p_own = send(cot_h, own_cot.at[:, lane], ps.at[0], pr.at[0], partner)
+    loads[2].wait()
+
+    def ring(rows, i, dev):
+        ref = own_cot.at[rows, lane]
+        return send(ref, ref, xs.at[i], xr.at[i], dev)
+
+    ra = ring(lo, 0, to_right)
+    lb = ring(hi, 1, to_left)
+    rb = ring(hi, 2, to_right)
+    la = ring(lo, 3, to_left)
+    p_own = send(own_cot.at[:, lane], own_cot.at[:, lane], ps.at[0], pr.at[0], partner)
+    for cp in loads[3:]:
+        cp.start()
+    parts_k[me] = pk_s[z]
+    parts_v[me] = pv_s[z]
 
     def find(s, _):
         def scan(j, found):
@@ -149,7 +160,6 @@
 
     y2 = []
     for kv, ref in enumerate((parts_k, parts_v)):
-        loads[kv].wait()
         for cp in z1[kv]:
             cp.wait_recv()
         rows = ref.at[pl.ds(y * Z, Z)]
@@ -164,7 +174,6 @@
     p_la = forward(left, lo, 1)
     p_rb = forward(right, hi, 2)
 
-    loads[2].wait()
     loads[5].wait()
     p_own.wait_recv()
     grad_att(x, first=True)
@@ -192,6 +201,16 @@
         for p in range(4):
             full[p, z] = pick[z, p]
         z3.append(copies)
+
+    for cp in loads[3:5] + loads[6:]:
+        cp.wait()
+
+    def own_head(h, _):
+        own = dot(kall[4:].reshape(ROWS, HEAD), q3[h], NT)
+        own = jnp.where(mask_s[...] != 0, own, MASKED)
+        so_s[h] = own
+        top_s[h] = jnp.max(own, 0, keepdims=True)
+        return 0
 
     rb.wait_recv()
     p_lb = forward(left, hi, 3)
@@ -207,26 +226,22 @@
     p_rb.wait_recv()
     p_ra.wait_recv()
     grad_att(right)
-
-    for cp in loads[3:5] + loads[6:]:
-        cp.wait()
+    lax.fori_loop(0, HEADS, own_head, 0, unroll=True)
+
+    def queries_of(h):
+        return pl.ds(pl.multiple_of(h * ROWS, ROWS), ROWS)
+
+    def features_of(h):
+        return pl.ds(pl.multiple_of(h * HEAD, HEAD), HEAD)
+
     for cp in z3[0]:
         cp.wait_recv()
-    kt_s[...] = kall[...].reshape(KEYS, HEAD).T
-
-    def queries_of(h):
-        return pl.ds(pl.multiple_of(h * ROWS, ROWS), ROWS)
-
-    def features_of(h):
-        return pl.ds(pl.multiple_of(h * HEAD, HEAD), HEAD)
 
     def score_head(h, _):
-        st = dot(kall[...].reshape(KEYS, HEAD), q3[h], NT)
-        s0 = st[:PROMPT]
-        s1 = jnp.where(mask_s[...] != 0, st[PROMPT:], MASKED)
-        top = jnp.maximum(jnp.max(s0, 0, keepdims=True), jnp.max(s1, 0, keepdims=True))
+        s0 = dot(kall[:4].reshape(PROMPT, HEAD), q3[h], NT)
+        top = jnp.maximum(jnp.max(s0, 0, keepdims=True), top_s[h])
         e0 = jnp.exp2((s0 - top) * EXP_SCALE)
-        e1 = jnp.exp2((s1 - top) * EXP_SCALE)
+        e1 = jnp.exp2((so_s[h] - top) * EXP_SCALE)
         total = jnp.sum(e0, 0, keepdims=True) + jnp.sum(e1, 0, keepdims=True)
         inverse_s[h] = 1.0 / total
         pt_s[:PROMPT, queries_of(h)] = e0.astype(BF16)
@@ -256,7 +271,7 @@
     lax.fori_loop(0, HEADS, value_head, 0, unroll=True)
 
     def reduce_start(kv, grad, g_ref, rg):
-        g_ref[...] = grad[:PROMPT].astype(BF16).reshape(4, Z, 16, HEAD)
+        g_ref[...] = grad.astype(BF16).reshape(4, Z, 16, HEAD)
         rg[z] = g_ref[:, z]
         return [
             send(
@@ -268,24 +283,28 @@
     b3 = [None, None]
     b2 = [None, None]
     b1 = [None, None]
-    grad_v = dot(pt_s[...], ga_n[...], NT)
-    b3[1] = reduce_start(1, grad_v, g_v, rg_v)
-    gkv_s[1] = grad_v[PROMPT:].astype(BF16)
-    stores = [pltpu.make_async_copy(gkv_s.at[1], gv_h, loc.at[14])]
-    stores[-1].start()
-
-    def backward_head(h, _):
-        grad_p = dot(vall[...].reshape(KEYS, HEAD), ga_n[:, queries_of(h)])
-        probs = pt_s[:, queries_of(h)].astype(F32)
-        ds_s[:, queries_of(h)] = (probs * (grad_p - delta_s[h])).astype(BF16)
-        return 0
-
-    lax.fori_loop(0, HEADS, backward_head, 0, unroll=True)
-    grad_k = dot(ds_s[...], q3[...].reshape(HEADS * ROWS, HEAD)) * SCALE
-    b3[0] = reduce_start(0, grad_k, g_k, rg_k)
-    gkv_s[0] = grad_k[PROMPT:].astype(BF16)
-    stores.append(pltpu.make_async_copy(gkv_s.at[0], gk_h, loc.at[15]))
-    stores[-1].start()
+    stores = []
+
+    def store(src, dst, i):
+        stores.append(pltpu.make_async_copy(src, dst, loc.at[i]))
+        stores[-1].start()
+
+    def score_grads(rows, values):
+        def head(h, _):
+            grad_p = dot(values, ga_n[:, queries_of(h)])
+            probs = pt_s[rows, queries_of(h)].astype(F32)
+            ds_s[rows, queries_of(h)] = (probs * (grad_p - delta_s[h])).astype(BF16)
+            return 0
+
+        lax.fori_loop(0, HEADS, head, 0, unroll=True)
+
+    prompt, own = slice(0, PROMPT), slice(PROMPT, KEYS)
+
+    def value_grads(rows):
+        return dot(pt_s[rows], ga_n[...], NT)
+
+    def key_grads(rows):
+        return dot(ds_s[rows], q3[...].reshape(HEADS * ROWS, HEAD)) * SCALE
 
     def query_head(h, _):
         dq = dot(kt_s[...], ds_s[:, queries_of(h)])
@@ -319,25 +338,18 @@
             for d in range(1, Y)
         ]
 
-    def reduce_y(kv, rq, u, fin):
+    def reduce_y(kv, rq, u, out):
         for cp in b2[kv]:
             cp.wait_recv()
         total = rq[0].astype(F32)
         for source in range(1, Y):
             total += rq[source].astype(F32)
         u[...] = total.astype(BF16)
-        fin[z] = u[z]
         b1[kv] = [
-            send(u.at[lax.rem(z + d, Z)], fin.at[z], b1s.at[kv, d], b1r.at[kv, d], at_z(d))
+            send(u.at[lax.rem(z + d, Z)], out.at[z], b1s.at[kv, d], b1r.at[kv, d], at_z(d))
             for d in range(1, Z)
         ]
-
-    def reduce_end(kv, fin, out, dst):
-        for cp in b1[kv]:
-            cp.wait_recv()
-        out[...] = fin[...].astype(F32)
-        stores.append(pltpu.make_async_copy(out, dst, loc.at[17 + kv]))
-        stores[-1].start()
+        store(u.at[z], out.at[z], 17 + kv)
 
     core = [None] * CH
     one = [None] * CH
@@ -373,52 +385,65 @@
         two[n][0].wait_recv()
         two[n][1].wait_recv()
         total = acc[n, 0].astype(F32) + rs2[n, 0].astype(F32) + rs2[n, 1].astype(F32)
-        bo_s[:, n * CW : (n + 1) * CW] = total.astype(BF16)
-
+        cols = pl.ds(n * CW, CW)
+        bo_s[:, cols] = total.astype(BF16)
+        store(bo_s.at[:, cols], bo_h.at[:, cols], 19 + n)
+
+    b3[1] = reduce_start(1, value_grads(prompt), g_v, rg_v)
+    score_grads(prompt, vall[:4].reshape(PROMPT, HEAD))
+    b3[0] = reduce_start(0, key_grads(prompt), g_k, rg_k)
     product(0)
     product(1)
+    product(2)
     ring_one(0)
-    product(2)
+    product(3)
     ring_one(1)
-    product(3)
-    lax.fori_loop(0, HEADS, query_head, 0, unroll=True)
-    stores.append(pltpu.make_async_copy(gq_s, gq_h, loc.at[16]))
-    stores[-1].start()
+    score_grads(own, vall[4:].reshape(ROWS, HEAD))
+    ring_one(2)
+    gkv_s[1] = value_grads(own).astype(BF16)
+    store(gkv_s.at[1], gv_h, 14)
+    kt_s[...] = kall[...].reshape(KEYS, HEAD).T
+    ring_one(3)
     reduce_z(1, rg_v, qs_v, rq_v)
-    ring_one(2)
-    ring_one(3)
     ring_two(0)
     reduce_z(0, rg_k, qs_k, rq_k)
     ring_two(1)
-    reduce_y(1, rq_v, u_v, fin_v)
+    gkv_s[0] = key_grads(own).astype(BF16)
+    store(gkv_s.at[0], gk_h, 15)
     ring_two(2)
+    lax.fori_loop(0, HEADS, query_head, 0, unroll=True)
+    store(gq_s, gq_h, 16)
     ring_two(3)
-    reduce_y(0, rq_k, u_k, fin_k)
-    early = len(sent)
-    for cp in sent[: early - 2 * Z]:
-        cp.wait_send()
+    reduce_y(1, rq_v, u_v, gpv_h)
+    reduce_y(0, rq_k, u_k, gpk_h)
     ring_end(0)
     ring_end(1)
-    reduce_end(1, fin_v, out_v, gpv_h)
+    late = 2 * Z - 2
+    for cp in sent[:-late]:
+        cp.wait_send()
     ring_end(2)
     ring_end(3)
-    stores.append(pltpu.make_async_copy(bo_s, bo_h, loc.at[19]))
-    stores[-1].start()
-    reduce_end(0, fin_k, out_k, gpk_h)
-    for cp in sent[early - 2 * Z :]:
+    for copies in (b1[1], b1[0]):
+        for cp in copies:
+            cp.wait_recv()
+    for cp in sent[-late:]:
         cp.wait_send()
     for cp in stores:
         cp.wait()
 
 
 def place(*refs):
-    ins, outs, held, (taken, given) = refs[:6], refs[6:12], refs[12:18], refs[18:]
+    ins, outs, held, wide = refs[:6], refs[6:12], refs[12:18], refs[18:20]
+    taken, given = refs[20:]
     loads = [pltpu.make_async_copy(a, b, taken.at[i]) for i, (a, b) in enumerate(zip(ins, held))]
-    stores = [pltpu.make_async_copy(a, b, given.at[i]) for i, (a, b) in enumerate(zip(held, outs))]
+    ready = held[:4] + wide
+    stores = [pltpu.make_async_copy(a, b, given.at[i]) for i, (a, b) in enumerate(zip(ready, outs))]
     for cp in loads:
         cp.start()
-    for load, store in zip(loads, stores):
+    for i, (load, store) in enumerate(zip(loads, stores)):
         load.wait()
+        if i >= 4:
+            wide[i - 4][...] = held[i][...].astype(F32)
         store.start()
     for cp in stores:
         cp.wait()
@@ -434,6 +459,8 @@
     dma = pltpu.SemaphoreType.DMA
     tile = (16, HEAD)
     scratch = [
+        vm((Z,) + tile, BF16),
+        vm((Z,) + tile, BF16),
         vm((HEADS * HEAD, D), BF16),
         vm((X, ROWS, PAIR), BF16),
         vm((HEADS * HEAD, ROWS), F32),
@@ -466,10 +493,8 @@
         vm((Y, Z) + tile, BF16),
         vm((Z,) + tile, BF16),
         vm((Z,) + tile, BF16),
-        vm((Z,) + tile, BF16),
-        vm((Z,) + tile, BF16),
-        vm((Z,) + tile, F32),
-        vm((Z,) + tile, F32),
+        vm((HEADS, ROWS, ROWS), F32),
+        vm((HEADS, 1, ROWS), F32),
         vm((CH, X, 2, 32, CW), BF16),
         vm((CH, X, 32, CW), BF16),
         vm((CH, X, 32, CW), BF16),
@@ -477,7 +502,7 @@
         vm((CH, 2, 32, CW), BF16),
         vm((32, D), BF16),
         pltpu.SMEM((Y * Z,), jnp.int32),
-        dma((20,)),
+        dma((19 + CH,)),
         dma((2, Z)), dma((2, Z)),
         dma((2, Y)), dma((2, Y)),
         dma((2, Z)), dma((2, Z)),
@@ -498,8 +523,8 @@
             shape((ROWS, HEADS * HEAD), BF16),
             shape((ROWS, HEAD), BF16),
             shape((ROWS, HEAD), BF16),
-            shape((Z,) + tile, F32),
-            shape((Z,) + tile, F32),
+            shape((Z,) + tile, BF16),
+            shape((Z,) + tile, BF16),
         ),
         in_specs=[smem] * 3 + [hbm] * 7,
         out_specs=[hbm] * 6,
@@ -520,12 +545,15 @@
         out_weight,
         cotangent,
     )
+    wide = shape((Z,) + tile, F32)
     outs = pl.pallas_call(
         place,
-        out_shape=tuple(shape(o.shape, o.dtype) for o in outs),
+        out_shape=tuple(shape(o.shape, o.dtype) for o in outs[:4]) + (wide, wide),
         in_specs=[hbm] * 6,
         out_specs=[hbm] * 6,
-        scratch_shapes=[vm(o.shape, o.dtype) for o in outs] + [dma((6,)), dma((6,))],
+        scratch_shapes=[vm(o.shape, o.dtype) for o in outs]
+        + [vm(wide.shape, F32)] * 2
+        + [dma((6,)), dma((6,))],
         name="place",
     )(*outs)
     return outs[:4] + (outs[4].reshape(128, HEAD), outs[5].reshape(128, HEAD))

time: 60 us -> 56.6 us (0.943)
  Pallas kernels: 59.2 us -> 55.6 us
    pallas_call x1, Pallas kernels: 57.1 us -> 53.5 us  [local(): pl.pallas_call(kernel, out_shape=(shape((32, D), BF16), shape((ROWS, HEAD...]
where the time goes in v1:
time: 56.6 us; the launch traced here: 56.4 us
  Pallas kernels  55.6 us (98%)
  between operations  0.8 us (1%)
    pallas_call x1, Pallas kernels, local(): pl.pallas_call(kernel, out_shape=(shape((32, D), BF16), shape((ROWS, HEAD...  53.5 us
    pallas_call x1, Pallas kernels, local(): pl.pallas_call(place, out_shape=tuple((shape(o.shape, o.dtype) for o in o...  2.12 us

profile of v1, /device:TPU:1, one launch (start us, length us, event | category | flops | bytes accessed | tf_op | source)
XLA Modules:
  0.0 56.4 jit_solution(2455350901636194579)
XLA Ops:
  0.6 53.5 %attention_block.1 = (bf16[32,5120]{1,0:T(8,128)(2,1)}, bf16[256,1024]{1,0:T(8,128)(2,1)}, bf16[256,128]{1,0:T(8,128)(2,1)}, bf16[256,128]{1,0:T(8,128)(2,1)}, b...) custom-call(s32[1,4]{1,0:T(1,128)} %len_s.1, s32[32]{0:T(128)} %own_s.1, s32[32]{0:T(128)} %grp_s.1, ...), custom_call_target="tpu_custom_call" | custom-call | tf_op jit(solution)/shard_map/attention_block/pallas_call | solution.py:519
  54.2 2.1 %place.1 = (bf16[32,5120]{1,0:T(8,128)(2,1)}, bf16[256,1024]{1,0:T(8,128)(2,1)}, bf16[256,128]{1,0:T(8,128)(2,1)}, bf16[256,128]{1,0:T(8,128)(2,1)}, f32[8,16,128]{2,1,0:T(8,128)}, /*index=5*/f32[8,16,128]{2,1,0:T(8,128)}) custom-call(bf16[32,5120]{1,0:T(8,128)(2,1)} %get-tuple-element.18.refs_0_, bf16[256,1024]{1,0:T(8,128)(2,1)} %get-tuple-element.19.refs_1_, ...), custom_call_target="tpu_custom_call" | custom-call | tf_op jit(solution)/shard_map/place/pallas_call | solution.py:549

commit v2 on v1

--- a/solution.py
+++ b/solution.py
@@ -35,12 +35,11 @@
     len_s, own_s, grp_s,
     q_h, k_h, v_h, pk_h, pv_h, w_h, cot_h,
     bo_h, gq_h, gk_h, gv_h, gpk_h, gpv_h,
-    pk_s, pv_s, w_s, cot_s, ga_acc, ga_t, q3, kall, vall, kt_s, vt_s, parts_k, parts_v, pick_k, pick_v,
+    pk_s, pv_s, w_s, cot_s, ga_acc, ga_t, q_s, q3, kall, vall, kt_s, vt_s, parts_k, parts_v, pick_k, pick_v,
     mask_s, pt_s, ds_s, ga_n, inverse_s, delta_s, att_s, gq_s, gkv_s,
     g_k, g_v, rg_k, rg_v, qs_k, qs_v, rq_k, rq_v, u_k, u_v, so_s, top_s,
     pb, rb1, acc, rs1, rs2, bo_s, inv_s,
-    loc, z1s, z1r, y2s, y2r, z3s, z3r, xs, xr, ps, pr,
-    b3s, b3r, b2s, b2r, b1s, b1r, cs, cr, r1s, r1r, r2s, r2r,
+    loc, zs, zr, xs, xr, ps, pr, cs, cr, r1s, r1r, r2s, r2r,
 ):
     me = lax.axis_index("dp")
     t = lax.axis_index("tensor")
@@ -59,15 +58,25 @@
     to_right = (me, right * 2 + c)
     to_left = (me, left * 2 + c)
     partner = (me, x * 2 + 1 - c)
-    sent = []
 
     def send(src, dst, ss, rs, dev):
         cp = pltpu.make_async_remote_copy(
             src_ref=src, dst_ref=dst, send_sem=ss, recv_sem=rs, device_id=dev, device_id_type=MESH
         )
         cp.start()
-        sent.append(cp)
         return cp
+
+    def arrived(ref, rs):
+        pltpu.make_async_remote_copy(
+            src_ref=ref, dst_ref=ref, send_sem=rs, recv_sem=rs, device_id=partner,
+            device_id_type=MESH,
+        ).wait_recv()
+
+    def left_here(ref, ss):
+        pltpu.make_async_remote_copy(
+            src_ref=ref, dst_ref=ref, send_sem=ss, recv_sem=ss, device_id=partner,
+            device_id_type=MESH,
+        ).wait_send()
 
     lane = pl.ds(pl.multiple_of(c * BLK, 128), BLK)
     loads = [
@@ -76,12 +85,9 @@
         pltpu.make_async_copy(cot_h, cot_s.at[x, :, lane], loc.at[0]),
         pltpu.make_async_copy(k_h, kall.at[pl.ds(4, 2)], loc.at[1]),
         pltpu.make_async_copy(v_h, vall.at[pl.ds(4, 2)], loc.at[2]),
+        pltpu.make_async_copy(q_h, q_s, loc.at[6]),
         pltpu.make_async_copy(w_h, w_s, loc.at[5]),
     ]
-    for h in range(HEADS):
-        loads.append(
-            pltpu.make_async_copy(q_h.at[:, pl.ds(h * HEAD, HEAD)], q3.at[h], loc.at[6 + h])
-        )
     for cp in loads[:3]:
         cp.start()
 
@@ -92,22 +98,17 @@
         pl.semaphore_signal(barrier, inc=1, device_id=dev, device_id_type=MESH)
     pl.semaphore_wait(barrier, len(peers))
 
-    z1 = []
     for kv, (src, dst) in enumerate(((pk_s, parts_k), (pv_s, parts_v))):
         loads[kv].wait()
-        z1.append(
-            [
-                send(src.at[lax.rem(z + d, Z)], dst.at[me], z1s.at[kv, d], z1r.at[kv, d], at_z(d))
-                for d in range(1, Z)
-            ]
-        )
+        for d in range(1, Z):
+            send(src.at[lax.rem(z + d, Z)], dst.at[me], zs.at[0, kv], zr.at[0, kv], at_z(d))
     lo, hi = pl.ds(0, 128), pl.ds(128, 128)
     own_cot = cot_s.at[x]
     loads[2].wait()
 
     def ring(rows, i, dev):
         ref = own_cot.at[rows, lane]
-        return send(ref, ref, xs.at[i], xr.at[i], dev)
+        return send(ref, ref, xs.at[0], xr.at[i], dev)
 
     ra = ring(lo, 0, to_right)
     lb = ring(hi, 1, to_left)
@@ -146,7 +147,7 @@
 
     def forward(block, rows, s):
         ref = cot_s.at[block, rows, lane]
-        return send(ref, ref, ps.at[s], pr.at[s], partner)
+        return send(ref, ref, ps.at[0], pr.at[s], partner)
 
     def grad_att(block, first=False, last=False):
         cols = pl.ds(pl.multiple_of(block * PAIR, 128), PAIR)
@@ -158,30 +159,27 @@
         else:
             ga_acc[...] += part
 
-    y2 = []
     for kv, ref in enumerate((parts_k, parts_v)):
-        for cp in z1[kv]:
-            cp.wait_recv()
+        arrived(ref.at[pl.ds(0, Z - 1)], zr.at[0, kv])
         rows = ref.at[pl.ds(y * Z, Z)]
-        y2.append([send(rows, rows, y2s.at[kv, d], y2r.at[kv, d], at_y(d)) for d in range(1, Y)])
+        for d in range(1, Y):
+            send(rows, rows, zs.at[1, kv], zr.at[1, kv], at_y(d))
 
     ra.wait_recv()
     ref = cot_s.at[left, lo, lane]
-    fr = send(ref, ref, xs.at[4], xr.at[4], to_right)
+    fr = send(ref, ref, xs.at[0], xr.at[4], to_right)
     lb.wait_recv()
     ref = cot_s.at[right, hi, lane]
-    fl = send(ref, ref, xs.at[5], xr.at[5], to_left)
+    fl = send(ref, ref, xs.at[0], xr.at[5], to_left)
     p_la = forward(left, lo, 1)
     p_rb = forward(right, hi, 2)
 
-    loads[5].wait()
+    loads[6].wait()
     p_own.wait_recv()
     grad_att(x, first=True)
 
-    z3 = []
     for kv, (ref, pick, full) in enumerate(((parts_k, pick_k, kall), (parts_v, pick_v, vall))):
-        for cp in y2[kv]:
-            cp.wait_recv()
+        arrived(ref.at[pl.ds(0, (Y - 1) * Z)], zr.at[1, kv])
 
         def choose(dest, _, ref=ref, pick=pick):
             first = grp_s[y * Z + dest] * 4
@@ -190,20 +188,16 @@
             return 0
 
         lax.fori_loop(0, Z, choose, 0, unroll=True)
-        copies = []
         for d in range(1, Z):
             dest = lax.rem(z + d, Z)
-            copies.append(
-                send(
-                    pick.at[dest], full.at[pl.ds(0, 4), z], z3s.at[kv, d], z3r.at[kv, d], at_z(d)
-                )
-            )
+            send(pick.at[dest], full.at[pl.ds(0, 4), z], zs.at[2, kv], zr.at[2, kv], at_z(d))
         for p in range(4):
             full[p, z] = pick[z, p]
-        z3.append(copies)
-
-    for cp in loads[3:5] + loads[6:]:
+
+    for cp in loads[3:6]:
         cp.wait()
+    for h in range(HEADS):
+        q3[h] = q_s[:, h * HEAD : (h + 1) * HEAD]
 
     def own_head(h, _):
         own = dot(kall[4:].reshape(ROWS, HEAD), q3[h], NT)
@@ -234,8 +228,7 @@
     def features_of(h):
         return pl.ds(pl.multiple_of(h * HEAD, HEAD), HEAD)
 
-    for cp in z3[0]:
-        cp.wait_recv()
+    arrived(kall.at[pl.ds(0, 4), pl.ds(0, Z - 1)], zr.at[2, 0])
 
     def score_head(h, _):
         s0 = dot(kall[:4].reshape(PROMPT, HEAD), q3[h], NT)
@@ -254,8 +247,7 @@
     p_ob.wait_recv()
     grad_att(opp, last=True)
 
-    for cp in z3[1]:
-        cp.wait_recv()
+    arrived(vall.at[pl.ds(0, 4), pl.ds(0, Z - 1)], zr.at[2, 1])
     vt_s[...] = vall[...].reshape(KEYS, HEAD).T
 
     def value_head(h, _):
@@ -273,16 +265,9 @@
     def reduce_start(kv, grad, g_ref, rg):
         g_ref[...] = grad.astype(BF16).reshape(4, Z, 16, HEAD)
         rg[z] = g_ref[:, z]
-        return [
-            send(
-                g_ref.at[:, lax.rem(z + d, Z)], rg.at[z], b3s.at[kv, d], b3r.at[kv, d], at_z(d)
-            )
-            for d in range(1, Z)
-        ]
-
-    b3 = [None, None]
-    b2 = [None, None]
-    b1 = [None, None]
+        for d in range(1, Z):
+            send(g_ref.at[:, lax.rem(z + d, Z)], rg.at[z], zs.at[3, kv], zr.at[3, kv], at_z(d))
+
     stores = []
 
     def store(src, dst, i):
@@ -312,8 +297,7 @@
         return 0
 
     def reduce_z(kv, rg, qs, rq):
-        for cp in b3[kv]:
-            cp.wait_recv()
+        arrived(rg.at[pl.ds(0, Z - 1)], zr.at[3, kv])
 
         def slot(j, _):
             s = own_s[j]
@@ -327,29 +311,19 @@
 
         lax.fori_loop(0, Y * Z, slot, 0, unroll=4)
         rq[y] = qs[pl.ds(y * Z, Z)]
-        b2[kv] = [
-            send(
-                qs.at[pl.ds(lax.rem(y + d, Y) * Z, Z)],
-                rq.at[y],
-                b2s.at[kv, d],
-                b2r.at[kv, d],
-                at_y(d),
-            )
-            for d in range(1, Y)
-        ]
+        for d in range(1, Y):
+            block = qs.at[pl.ds(lax.rem(y + d, Y) * Z, Z)]
+            send(block, rq.at[y], zs.at[4, kv], zr.at[4, kv], at_y(d))
 
     def reduce_y(kv, rq, u, out):
-        for cp in b2[kv]:
-            cp.wait_recv()
+        arrived(rq.at[pl.ds(0, Y - 1)], zr.at[4, kv])
         total = rq[0].astype(F32)
         for source in range(1, Y):
             total += rq[source].astype(F32)
         u[...] = total.astype(BF16)
-        b1[kv] = [
-            send(u.at[lax.rem(z + d, Z)], out.at[z], b1s.at[kv, d], b1r.at[kv, d], at_z(d))
-            for d in range(1, Z)
-        ]
-        store(u.at[z], out.at[z], 17 + kv)
+        for d in range(1, Z):
+            send(u.at[lax.rem(z + d, Z)], out.at[z], zs.at[5, kv], zr.at[5, kv], at_z(d))
+        store(u.at[z], out.at[z], 10 + kv)
 
     core = [None] * CH
     one = [None] * CH
@@ -358,7 +332,7 @@
     def product(n):
         part = dot(att_s[...], w_s[:, n * CW : (n + 1) * CW])
         pb[n] = part.astype(BF16).reshape(X, 2, 32, CW)
-        core[n] = send(pb.at[n, :, 1 - c], rb1.at[n], cs.at[n], cr.at[n], partner)
+        core[n] = send(pb.at[n, :, 1 - c], rb1.at[n], cs.at[0], cr.at[n], partner)
 
     def ring_one(n):
         core[n].wait_recv()
@@ -366,19 +340,19 @@
             b = lax.rem(x + d, X)
             acc[n, d] = (pb[n, b, c].astype(F32) + rb1[n, b].astype(F32)).astype(BF16)
         one[n] = (
-            send(acc.at[n, 2, pl.ds(0, 16)], rs1.at[n, 0], r1s.at[n, 0], r1r.at[n, 0], to_right),
-            send(acc.at[n, 2, pl.ds(16, 16)], rs1.at[n, 1], r1s.at[n, 1], r1r.at[n, 1], to_left),
+            send(acc.at[n, 2, pl.ds(0, 16)], rs1.at[n, 0], r1s.at[0], r1r.at[n, 0], to_right),
+            send(acc.at[n, 2, pl.ds(16, 16)], rs1.at[n, 1], r1s.at[0], r1r.at[n, 1], to_left),
         )
 
     def ring_two(n):
         one[n][0].wait_recv()
         acc[n, 1, :16] = (acc[n, 1, :16].astype(F32) + rs1[n, 0].astype(F32)).astype(BF16)
-        first = send(acc.at[n, 1], rs2.at[n, 0], r2s.at[n, 0], r2r.at[n, 0], to_right)
+        first = send(acc.at[n, 1], rs2.at[n, 0], r2s.at[0], r2r.at[n, 0], to_right)
         one[n][1].wait_recv()
         acc[n, 3, 16:] = (acc[n, 3, 16:].astype(F32) + rs1[n, 1].astype(F32)).astype(BF16)
         two[n] = (
             first,
-            send(acc.at[n, 3], rs2.at[n, 1], r2s.at[n, 1], r2r.at[n, 1], to_left),
+            send(acc.at[n, 3], rs2.at[n, 1], r2s.at[0], r2r.at[n, 1], to_left),
         )
 
     def ring_end(n):
@@ -387,11 +361,11 @@
         total = acc[n, 0].astype(F32) + rs2[n, 0].astype(F32) + rs2[n, 1].astype(F32)
         cols = pl.ds(n * CW, CW)
         bo_s[:, cols] = total.astype(BF16)
-        store(bo_s.at[:, cols], bo_h.at[:, cols], 19 + n)
-
-    b3[1] = reduce_start(1, value_grads(prompt), g_v, rg_v)
+        store(bo_s.at[:, cols], bo_h.at[:, cols], 12 + n)
+
+    reduce_start(1, value_grads(prompt), g_v, rg_v)
     score_grads(prompt, vall[:4].reshape(PROMPT, HEAD))
-    b3[0] = reduce_start(0, key_grads(prompt), g_k, rg_k)
+    reduce_start(0, key_grads(prompt), g_k, rg_k)
     product(0)
     product(1)
     product(2)
@@ -401,7 +375,7 @@
     score_grads(own, vall[4:].reshape(ROWS, HEAD))
     ring_one(2)
     gkv_s[1] = value_grads(own).astype(BF16)
-    store(gkv_s.at[1], gv_h, 14)
+    store(gkv_s.at[1], gv_h, 7)
     kt_s[...] = kall[...].reshape(KEYS, HEAD).T
     ring_one(3)
     reduce_z(1, rg_v, qs_v, rq_v)
@@ -409,25 +383,31 @@
     reduce_z(0, rg_k, qs_k, rq_k)
     ring_two(1)
     gkv_s[0] = key_grads(own).astype(BF16)
-    store(gkv_s.at[0], gk_h, 15)
+    store(gkv_s.at[0], gk_h, 8)
     ring_two(2)
     lax.fori_loop(0, HEADS, query_head, 0, unroll=True)
-    store(gq_s, gq_h, 16)
+    store(gq_s, gq_h, 9)
     ring_two(3)
     reduce_y(1, rq_v, u_v, gpv_h)
     reduce_y(0, rq_k, u_k, gpk_h)
     ring_end(0)
     ring_end(1)
-    late = 2 * Z - 2
-    for cp in sent[:-late]:
-        cp.wait_send()
+    for kv in range(2):
+        left_here(parts_k.at[pl.ds(0, Z - 1)], zs.at[0, kv])
+        left_here(parts_k.at[pl.ds(0, (Y - 1) * Z)], zs.at[1, kv])
+        left_here(pick_k.at[pl.ds(0, Z - 1)], zs.at[2, kv])
+        left_here(rg_k.at[pl.ds(0, Z - 1)], zs.at[3, kv])
+        left_here(rq_k.at[pl.ds(0, Y - 1)], zs.at[4, kv])
+    left_here(cot_s.at[pl.ds(0, 3), :, pl.ds(0, BLK)], xs.at[0])
+    left_here(cot_s.at[:, :, pl.ds(0, BLK)], ps.at[0])
+    left_here(rb1, cs.at[0])
+    left_here(rs1, r1s.at[0])
     ring_end(2)
     ring_end(3)
-    for copies in (b1[1], b1[0]):
-        for cp in copies:
-            cp.wait_recv()
-    for cp in sent[-late:]:
-        cp.wait_send()
+    left_here(rs2, r2s.at[0])
+    for kv, (u, out) in ((1, (u_v, gpv_h)), (0, (u_k, gpk_h))):
+        arrived(out.at[pl.ds(0, Z - 1)], zr.at[5, kv])
+        left_here(u.at[pl.ds(0, Z - 1)], zs.at[5, kv])
     for cp in stores:
         cp.wait()
 
@@ -465,6 +445,7 @@
         vm((X, ROWS, PAIR), BF16),
         vm((HEADS * HEAD, ROWS), F32),
         vm((HEADS, HEAD, ROWS), BF16),
+        vm((ROWS, HEADS * HEAD), BF16),
         vm((HEADS, ROWS, HEAD), BF16),
         vm((6, Z) + tile, BF16),
         vm((6, Z) + tile, BF16),
@@ -502,18 +483,13 @@
         vm((CH, 2, 32, CW), BF16),
         vm((32, D), BF16),
         pltpu.SMEM((Y * Z,), jnp.int32),
-        dma((19 + CH,)),
-        dma((2, Z)), dma((2, Z)),
-        dma((2, Y)), dma((2, Y)),
-        dma((2, Z)), dma((2, Z)),
-        dma((6,)), dma((6,)),
-        dma((7,)), dma((7,)),
-        dma((2, Z)), dma((2, Z)),
-        dma((2, Y)), dma((2, Y)),
-        dma((2, Z)), dma((2, Z)),
-        dma((CH,)), dma((CH,)),
-        dma((CH, 2)), dma((CH, 2)),
-        dma((CH, 2)), dma((CH, 2)),
+        dma((16,)),
+        dma((6, 2)), dma((6, 2)),
+        dma((1,)), dma((6,)),
+        dma((1,)), dma((7,)),
+        dma((1,)), dma((CH,)),
+        dma((1,)), dma((CH, 2)),
+        dma((1,)), dma((CH, 2)),
     ]
     shape = jax.ShapeDtypeStruct
     outs = pl.pallas_call(

time: 56.6 us -> 54.9 us (0.970)
  Pallas kernels: 55.6 us -> 54.1 us
    pallas_call x1, Pallas kernels: 53.5 us -> 52 us  [local(): pl.pallas_call(kernel, out_shape=(shape((32, D), BF16), shape((ROWS, HEAD...]
where the time goes in v2:
time: 54.9 us; the launch traced here: 54.7 us
  Pallas kernels  54.1 us (99%)
  between operations  0.64 us (1%)
    pallas_call x1, Pallas kernels, local(): pl.pallas_call(kernel, out_shape=(shape((32, D), BF16), shape((ROWS, HEAD...  52 us
    pallas_call x1, Pallas kernels, local(): pl.pallas_call(place, out_shape=tuple((shape(o.shape, o.dtype) for o in o...  2.12 us

profile of v2, /device:TPU:1, one launch (start us, length us, event | category | flops | bytes accessed | tf_op | source)
XLA Modules:
  0.0 54.7 jit_solution(9410408481389578938)
XLA Ops:
  0.6 52.0 %attention_block.1 = (bf16[32,5120]{1,0:T(8,128)(2,1)}, bf16[256,1024]{1,0:T(8,128)(2,1)}, bf16[256,128]{1,0:T(8,128)(2,1)}, bf16[256,128]{1,0:T(8,128)(2,1)}, b...) custom-call(s32[1,4]{1,0:T(1,128)} %len_s.1, s32[32]{0:T(128)} %own_s.1, s32[32]{0:T(128)} %grp_s.1, ...), custom_call_target="tpu_custom_call" | custom-call | tf_op jit(solution)/shard_map/attention_block/pallas_call | solution.py:495
  52.6 2.1 %place.1 = (bf16[32,5120]{1,0:T(8,128)(2,1)}, bf16[256,1024]{1,0:T(8,128)(2,1)}, bf16[256,128]{1,0:T(8,128)(2,1)}, bf16[256,128]{1,0:T(8,128)(2,1)}, f32[8,16,128]{2,1,0:T(8,128)}, /*index=5*/f32[8,16,128]{2,1,0:T(8,128)}) custom-call(bf16[32,5120]{1,0:T(8,128)(2,1)} %get-tuple-element.18.refs_0_, bf16[256,1024]{1,0:T(8,128)(2,1)} %get-tuple-element.19.refs_1_, ...), custom_call_target="tpu_custom_call" | custom-call | tf_op jit(solution)/shard_map/place/pallas_call | solution.py:525

commit v3 on v2

--- a/solution.py
+++ b/solution.py
@@ -151,13 +151,21 @@
 
     def grad_att(block, first=False, last=False):
         cols = pl.ds(pl.multiple_of(block * PAIR, 128), PAIR)
-        part = dot(w_s[:, cols], cot_s[block], NT)
-        if first:
-            ga_acc[...] = part
-        elif last:
-            ga_t[...] = (ga_acc[...] + part).astype(BF16).reshape(HEADS, HEAD, ROWS)
-        else:
-            ga_acc[...] += part
+
+        def step(i, _):
+            rows = pl.ds(pl.multiple_of(i * 512, 512), 512)
+            part = dot(w_s[rows, cols], cot_s[block], NT)
+            if first:
+                ga_acc[rows, :] = part
+            elif last:
+                ga_t[pl.ds(i * 4, 4)] = (
+                    (ga_acc[rows, :] + part).astype(BF16).reshape(HEADS // 2, HEAD, ROWS)
+                )
+            else:
+                ga_acc[rows, :] += part
+            return 0
+
+        lax.fori_loop(0, 2, step, 0)
 
     for kv, ref in enumerate((parts_k, parts_v)):
         arrived(ref.at[pl.ds(0, Z - 1)], zr.at[0, kv])
@@ -187,7 +195,7 @@
                 pick[dest, p] = ref[inv_s[first + p]]
             return 0
 
-        lax.fori_loop(0, Z, choose, 0, unroll=True)
+        lax.fori_loop(0, Z, choose, 0, unroll=4)
         for d in range(1, Z):
             dest = lax.rem(z + d, Z)
             send(pick.at[dest], full.at[pl.ds(0, 4), z], zs.at[2, kv], zr.at[2, kv], at_z(d))
@@ -206,6 +214,7 @@
         top_s[h] = jnp.max(own, 0, keepdims=True)
         return 0
 
+    lax.fori_loop(0, HEADS, own_head, 0, unroll=4)
     rb.wait_recv()
     p_lb = forward(left, hi, 3)
     la.wait_recv()
@@ -220,8 +229,6 @@
     p_rb.wait_recv()
     p_ra.wait_recv()
     grad_att(right)
-    lax.fori_loop(0, HEADS, own_head, 0, unroll=True)
-
     def queries_of(h):
         return pl.ds(pl.multiple_of(h * ROWS, ROWS), ROWS)
 
@@ -241,7 +248,7 @@
         pt_s[PROMPT:, queries_of(h)] = e1.astype(BF16)
         return 0
 
-    lax.fori_loop(0, HEADS, score_head, 0, unroll=True)
+    lax.fori_loop(0, HEADS, score_head, 0, unroll=4)
 
     p_oa.wait_recv()
     p_ob.wait_recv()
@@ -260,7 +267,7 @@
         att_s[:, features_of(h)] = out_t.T.astype(BF16)
         return 0
 
-    lax.fori_loop(0, HEADS, value_head, 0, unroll=True)
+    lax.fori_loop(0, HEADS, value_head, 0, unroll=4)
 
     def reduce_start(kv, grad, g_ref, rg):
         g_ref[...] = grad.astype(BF16).reshape(4, Z, 16, HEAD)
@@ -281,7 +288,7 @@
             ds_s[rows, queries_of(h)] = (probs * (grad_p - delta_s[h])).astype(BF16)
             return 0
 
-        lax.fori_loop(0, HEADS, head, 0, unroll=True)
+        lax.fori_loop(0, HEADS, head, 0, unroll=4)
 
     prompt, own = slice(0, PROMPT), slice(PROMPT, KEYS)
 
@@ -330,8 +337,15 @@
     two = [None] * CH
 
     def product(n):
-        part = dot(att_s[...], w_s[:, n * CW : (n + 1) * CW])
-        pb[n] = part.astype(BF16).reshape(X, 2, 32, CW)
+        half = CW // 2
+
+        def step(i, _):
+            cols = pl.ds(pl.multiple_of(n * CW + i * half, 128), half)
+            part = dot(att_s[...], w_s[:, cols]).astype(BF16)
+            pb[n, :, :, :, pl.ds(pl.multiple_of(i * half, 128), half)] = part.reshape(X, 2, 32, half)
+            return 0
+
+        lax.fori_loop(0, 2, step, 0)
         core[n] = send(pb.at[n, :, 1 - c], rb1.at[n], cs.at[0], cr.at[n], partner)
 
     def ring_one(n):
@@ -368,24 +382,24 @@
     reduce_start(0, key_grads(prompt), g_k, rg_k)
     product(0)
     product(1)
+    ring_one(0)
     product(2)
-    ring_one(0)
+    ring_one(1)
     product(3)
-    ring_one(1)
+    ring_one(2)
     score_grads(own, vall[4:].reshape(ROWS, HEAD))
-    ring_one(2)
-    gkv_s[1] = value_grads(own).astype(BF16)
-    store(gkv_s.at[1], gv_h, 7)
-    kt_s[...] = kall[...].reshape(KEYS, HEAD).T
+    reduce_z(1, rg_v, qs_v, rq_v)
     ring_one(3)
-    reduce_z(1, rg_v, qs_v, rq_v)
     ring_two(0)
     reduce_z(0, rg_k, qs_k, rq_k)
+    kt_s[...] = kall[...].reshape(KEYS, HEAD).T
     ring_two(1)
     gkv_s[0] = key_grads(own).astype(BF16)
     store(gkv_s.at[0], gk_h, 8)
     ring_two(2)
-    lax.fori_loop(0, HEADS, query_head, 0, unroll=True)
+    gkv_s[1] = value_grads(own).astype(BF16)
+    store(gkv_s.at[1], gv_h, 7)
+    lax.fori_loop(0, HEADS, query_head, 0, unroll=4)
     store(gq_s, gq_h, 9)
     ring_two(3)
     reduce_y(1, rq_v, u_v, gpv_h)

time: 54.9 us -> 54.5 us (level)
  no operation moved by 1% of the time
where the time goes in v3:
time: 54.5 us; the launch traced here: 54.3 us
  Pallas kernels  53.7 us (99%)
  between operations  0.64 us (1%)
    pallas_call x1, Pallas kernels, local(): pl.pallas_call(kernel, out_shape=(shape((32, D), BF16), shape((ROWS, HEAD...  51.6 us
    pallas_call x1, Pallas kernels, local(): pl.pallas_call(place, out_shape=tuple((shape(o.shape, o.dtype) for o in o...  2.12 us

profile of v3, /device:TPU:1, one launch (start us, length us, event | category | flops | bytes accessed | tf_op | source)
XLA Modules:
  0.0 54.3 jit_solution(6102981442385103656)
XLA Ops:
  0.6 51.6 %attention_block.1 = (bf16[32,5120]{1,0:T(8,128)(2,1)}, bf16[256,1024]{1,0:T(8,128)(2,1)}, bf16[256,128]{1,0:T(8,128)(2,1)}, bf16[256,128]{1,0:T(8,128)(2,1)}, b...) custom-call(s32[1,4]{1,0:T(1,128)} %len_s.1, s32[32]{0:T(128)} %own_s.1, s32[32]{0:T(128)} %grp_s.1, ...), custom_call_target="tpu_custom_call" | custom-call | tf_op jit(solution)/shard_map/attention_block/pallas_call | solution.py:509
  52.2 2.1 %place.1 = (bf16[32,5120]{1,0:T(8,128)(2,1)}, bf16[256,1024]{1,0:T(8,128)(2,1)}, bf16[256,128]{1,0:T(8,128)(2,1)}, bf16[256,128]{1,0:T(8,128)(2,1)}, f32[8,16,128]{2,1,0:T(8,128)}, /*index=5*/f32[8,16,128]{2,1,0:T(8,128)}) custom-call(bf16[32,5120]{1,0:T(8,128)(2,1)} %get-tuple-element.18.refs_0_, bf16[256,1024]{1,0:T(8,128)(2,1)} %get-tuple-element.19.refs_1_, ...), custom_call_target="tpu_custom_call" | custom-call | tf_op jit(solution)/shard_map/place/pallas_call | solution.py:539

commit v4 on v3

--- a/solution.py
+++ b/solution.py
@@ -78,6 +78,11 @@
             device_id_type=MESH,
         ).wait_send()
 
+    barrier = pltpu.get_barrier_semaphore()
+    peers = [at_z(d) for d in range(1, Z)] + [at_y(d) for d in range(1, Y)]
+    peers += [to_right, to_left, partner]
+    for dev in peers:
+        pl.semaphore_signal(barrier, inc=1, device_id=dev, device_id_type=MESH)
     lane = pl.ds(pl.multiple_of(c * BLK, 128), BLK)
     loads = [
         pltpu.make_async_copy(pk_h, pk_s, loc.at[3]),
@@ -91,11 +96,6 @@
     for cp in loads[:3]:
         cp.start()
 
-    barrier = pltpu.get_barrier_semaphore()
-    peers = [at_z(d) for d in range(1, Z)] + [at_y(d) for d in range(1, Y)]
-    peers += [to_right, to_left, partner]
-    for dev in peers:
-        pl.semaphore_signal(barrier, inc=1, device_id=dev, device_id_type=MESH)
     pl.semaphore_wait(barrier, len(peers))
 
     for kv, (src, dst) in enumerate(((pk_s, parts_k), (pv_s, parts_v))):
@@ -248,7 +248,7 @@
         pt_s[PROMPT:, queries_of(h)] = e1.astype(BF16)
         return 0
 
-    lax.fori_loop(0, HEADS, score_head, 0, unroll=4)
+    lax.fori_loop(0, HEADS, score_head, 0, unroll=True)
 
     p_oa.wait_recv()
     p_ob.wait_recv()

time: 54.5 us -> 54.2 us (level)
  no operation moved by 1% of the time
where the time goes in v4:
time: 54.2 us; the launch traced here: 54.1 us
  Pallas kernels  53.5 us (99%)
  between operations  0.64 us (1%)
    pallas_call x1, Pallas kernels, local(): pl.pallas_call(kernel, out_shape=(shape((32, D), BF16), shape((ROWS, HEAD...  51.4 us
    pallas_call x1, Pallas kernels, local(): pl.pallas_call(place, out_shape=tuple((shape(o.shape, o.dtype) for o in o...  2.12 us

profile of v4, /device:TPU:1, one launch (start us, length us, event | category | flops | bytes accessed | tf_op | source)
XLA Modules:
  0.0 54.1 jit_solution(8793940804113863057)
XLA Ops:
  0.6 51.4 %attention_block.1 = (bf16[32,5120]{1,0:T(8,128)(2,1)}, bf16[256,1024]{1,0:T(8,128)(2,1)}, bf16[256,128]{1,0:T(8,128)(2,1)}, bf16[256,128]{1,0:T(8,128)(2,1)}, b...) custom-call(s32[1,4]{1,0:T(1,128)} %len_s.1, s32[32]{0:T(128)} %own_s.1, s32[32]{0:T(128)} %grp_s.1, ...), custom_call_target="tpu_custom_call" | custom-call | tf_op jit(solution)/shard_map/attention_block/pallas_call | solution.py:509
  52.0 2.1 %place.1 = (bf16[32,5120]{1,0:T(8,128)(2,1)}, bf16[256,1024]{1,0:T(8,128)(2,1)}, bf16[256,128]{1,0:T(8,128)(2,1)}, bf16[256,128]{1,0:T(8,128)(2,1)}, f32[8,16,128]{2,1,0:T(8,128)}, /*index=5*/f32[8,16,128]{2,1,0:T(8,128)}) custom-call(bf16[32,5120]{1,0:T(8,128)(2,1)} %get-tuple-element.18.refs_0_, bf16[256,1024]{1,0:T(8,128)(2,1)} %get-tuple-element.19.refs_1_, ...), custom_call_target="tpu_custom_call" | custom-call | tf_op jit(solution)/shard_map/place/pallas_call | solution.py:539
